TPU v7x, 32 devices: a whole 2x2x4 slice. The times are simulated.
32 devices in a mesh: wide: 32 (over z, y, x, core), narrow: 1.
Axes of the slice: x: 2, y: 2, z: 4, core: 2. Of those that a mesh axis runs over, the one named last changes fastest.
Arguments:
- field: float32 [256, 44, 512], P('wide', 'narrow')
- sketch_one: float32 [512, 128], replicated, may hold values from -6 to 6
- sketch_two: float32 [256, 128], replicated, may hold values from -6 to 6
- ranks: int32 [2], replicated, may hold values from 64 to 128, as said below
Outputs:
- core: float32 [128, 44, 128], P('wide', 'narrow')
Inputs may be any that keep to these rules, and one draw needn't show every extreme that they name: One of the two ranks equals 128.
All inputs are finite; a program needn't handle non-finite values.
Results may differ from a plain program's by a relative error of at most 0.00022.
Values sent between devices are 32-bit elements; how exact they have to be, the bound alone decides.
A program may use at most 64 MiB of HBM per device.

v0:
```python
import jax
import jax.numpy as jnp
from jax import lax
from jax.sharding import PartitionSpec as P


def combine(partial_sum):
    return lax.psum(partial_sum, ("wide", "narrow"))


def make_basis(local, sketch, rank):
    highest = lax.Precision.HIGHEST
    keep = (jnp.arange(sketch.shape[1]) < rank).astype(jnp.float32)
    masked = sketch * keep
    partial_gram = jnp.einsum("akn,akm->nm", local, local, precision=highest)
    sketched = jnp.dot(combine(partial_gram), masked, precision=highest)
    inner = jnp.dot(sketched.T, sketched, precision=highest) + jnp.diag(1.0 - keep)
    lower = jnp.linalg.cholesky(inner)
    return jax.scipy.linalg.solve_triangular(lower, sketched.T, lower=True)


def per_device(field, sketch_one, sketch_two, ranks):
    highest = lax.Precision.HIGHEST
    basis_one = make_basis(field, sketch_one, ranks[0])
    core_one = jnp.einsum("rn,ykn->rky", basis_one, field, precision=highest)
    regrouped = lax.all_to_all(core_one, "wide", split_axis=0, concat_axis=2, tiled=True)
    basis_two = make_basis(regrouped, sketch_two, ranks[1])
    return jnp.einsum("sn,rkn->rks", basis_two, regrouped, precision=highest)


def solution(mesh):
    return jax.shard_map(
        per_device,
        mesh=mesh,
        in_specs=(P("wide", "narrow", None), P(), P(), P()),
        out_specs=P("wide", "narrow", None),
        check_vma=False,
    )
```

profile of v0, /device:TPU:0, one launch (start us, length us, event | category | flops | bytes accessed | tf_op | source)
XLA Modules:
  0.0 346.2 jit_solution(5141929274860126565)
XLA Ops:
  6.5 0.0 copy-start
  6.5 0.0 all-reduce.3.cloned.1.call-start
  6.5 1.1 copy-done
  7.6 2.9 convolution_bitcast_fusion
  10.5 0.0 copy-start.3
  10.5 0.0 copy-start.1
  10.5 0.0 all-reduce.3.cloned.1.call-update
  10.6 0.0 all-reduce.5.cloned.1.call-start
  10.6 0.6 copy-done.3
  11.2 0.6 fusion.20
  11.8 0.6 compare_convert_fusion.1
  12.4 0.6 broadcast_subtract_fusion.1
  13.0 132.1 %all-reduce.3.cloned.1.call-done = f32[512,512]{1,0:T(8,128)} async-done(((f32[512,512]{1,0:T(8,128)}), f32[512,512]{1,0:T(8,128)}) %all-reduce.3.cloned.1.call-update) | async-done | bytes 1048592 | tf_op jit(solution)/shard_map/psum | solution.py:8
  145.2 0.0 copy-done.1
  145.2 2.2 fusion.6
  147.4 0.6 convolution_add_fusion.1
  148.0 0.1 copy.21
  148.1 0.1 copy.22
  148.2 11.7 %cholesky.44 = f32[128,128]{1,0:T(8,128)S(1)} custom-call(f32[128,128]{1,0:T(8,128)S(1)} %copy.22), custom_call_target="Cholesky" | custom-call | tf_op jit(solution)/shard_map/jit(cholesky)/cholesky | solution.py:18
  159.9 0.7 compare_reduce_fusion.1
  160.7 0.7 fusion.11
  161.4 9.8 %custom-call.10 = f32[1,128,128]{1,2,0:T(8,128)S(1)} custom-call(f32[1,128,128]{2,1,0:T(8,128)S(1)} %fusion.11), custom_call_target="InvertDiagBlocksLowerTriangular" | custom-call | tf_op jit(solution)/shard_map/jit(_solve_triangular)/triangular_solve | solution.py:19
  171.2 0.4 convolution_bitcast_fusion.2
  171.6 1.1 convolution_bitcast_fusion.3
  172.7 0.2 copy.24
  172.9 0.6 reshape.39
  173.6 12.1 %all_to_all.18 = f32[32,1,1408]{2,1,0:T(1,128)S(1)} all-to-all(f32[32,1,1408]{2,1,0:T(1,128)S(1)} %reshape.39), channel_id=1, replica_groups=mesh['wide'=32,'narrow'=1] {'wide'}, dimensions={0} | all-to-all | bytes 360448 | tf_op jit(solution)/shard_map/all_to_all | solution.py:26
  185.7 0.6 broadcast.90
  186.3 1.1 reduce.4
  187.4 0.7 reshape.40
  188.1 1.3 convolution_bitcast_fusion.1
  189.4 0.0 copy-start.2
  189.4 0.0 all-reduce.5.cloned.1.call-update
  189.4 0.7 compare_convert_fusion
  190.1 0.7 broadcast_subtract_fusion
  190.8 121.8 %all-reduce.5.cloned.1.call-done = f32[256,256]{1,0:T(8,128)} async-done(((f32[256,256]{1,0:T(8,128)}), f32[256,256]{1,0:T(8,128)}) %all-reduce.5.cloned.1.call-update) | async-done | bytes 262160 | tf_op jit(solution)/shard_map/psum | solution.py:8
  312.6 0.0 copy-done.2
  312.6 1.3 fusion.8
  313.9 0.4 convolution_add_fusion
  314.3 0.1 copy.28
  314.4 0.1 copy.29
  314.5 11.7 %cholesky.55 = f32[128,128]{1,0:T(8,128)S(1)} custom-call(f32[128,128]{1,0:T(8,128)S(1)} %copy.29), custom_call_target="Cholesky" | custom-call | tf_op jit(solution)/shard_map/jit(cholesky)/cholesky | solution.py:18
  326.3 0.6 compare_reduce_fusion
  326.9 0.7 fusion.12
  327.6 9.8 %custom-call.11 = f32[1,128,128]{1,2,0:T(8,128)S(1)} custom-call(f32[1,128,128]{2,1,0:T(8,128)S(1)} %fusion.12), custom_call_target="InvertDiagBlocksLowerTriangular" | custom-call | tf_op jit(solution)/shard_map/jit(_solve_triangular)/triangular_solve | solution.py:19
  337.4 0.3 convolution_bitcast_fusion.4
  337.7 1.0 fusion.1
  338.7 0.7 copy.31
  (4 shorter events, 0.1 us)
Async XLA Ops:
  6.5 1.1 copy-start
  6.5 138.6 %all-reduce.3.cloned.1.call-start = ((), (), s32[]{:S(2)}) async-start(), calls=%async_computation.1 | async-start | bytes 2097152 | tf_op jit(solution)/shard_map/psum | solution.py:8
  10.5 0.7 copy-start.3
  10.5 134.6 %copy-start.1 = (f32[512,128]{1,0:T(8,128)S(1)}, f32[512,128]{1,0:T(8,128)}, u32[]{:S(2)}) copy-start(f32[512,128]{1,0:T(8,128)} %param.6) | copy-start | bytes 786436
  10.6 302.0 %all-reduce.5.cloned.1.call-start = ((), (), s32[]{:S(2)}) async-start(), calls=%async_computation.2 | async-start | bytes 524288 | tf_op jit(solution)/shard_map/psum | solution.py:8
  189.4 123.2 %copy-start.2 = (f32[256,128]{1,0:T(8,128)S(1)}, f32[256,128]{1,0:T(8,128)}, u32[]{:S(2)}) copy-start(f32[256,128]{1,0:T(8,128)} %param.7) | copy-start | bytes 393220
Sparse Core Ops, SparseCore 0:
  12.5 132.5 all-reduce.2
  189.5 122.9 all-reduce.4
where the time goes:
time: 347 us; the launch traced here: 346 us
  waiting for transfers between devices  254 us (73%)
  other arithmetic  49.5 us (14%)
  between operations  13.6 us (4%)
  blocking collectives  12.1 us (3%)
  matrix products  11.5 us (3%)
  local copies, waits for them, and re-layouts  5.47 us (2%)
    psum x2, waiting for transfers between devices, combine(): return lax.psum(partial_sum, ('wide', 'narrow'))  254 us
    another operation x6, other arithmetic, make_basis(): lower = jnp.linalg.cholesky(inner)  24.9 us
    another operation x4, other arithmetic, make_basis(): return jax.scipy.linalg.solve_triangular(lower, sketched.T, lower=True)  21 us
    all_to_all x1, blocking collectives, per_device(): lax.all_to_all(core_one, 'wide', split_axis=0, concat_axis=2, tiled=True)  12.1 us
  transfers between devices with their start and end apart: 2, of which 2 were waited for; matrix products, arithmetic and copies ran while one was open for 1% of the time, Pallas kernels for 0%

commit v1 on v0

v1 whole, which is shorter than its diff:
```python
import functools

import jax
import jax.numpy as jnp
from jax import lax
from jax.experimental import pallas as pl
from jax.experimental.pallas import tpu as pltpu
from jax.sharding import PartitionSpec as P

HIGHEST = lax.Precision.HIGHEST
MESH = pl.DeviceIdType.MESH


def make_basis(local, sketch, rank):
    keep = (jnp.arange(sketch.shape[1]) < rank).astype(jnp.float32)
    masked = sketch * keep
    part = jnp.einsum("akn,ns->aks", local, masked, precision=HIGHEST)
    part = jnp.einsum("akn,aks->ns", local, part, precision=HIGHEST)
    sketched = lax.psum(part, ("wide", "narrow"))
    inner = jnp.dot(sketched.T, sketched, precision=HIGHEST) + jnp.diag(1.0 - keep)
    lower = jnp.linalg.cholesky(inner)
    return jax.scipy.linalg.solve_triangular(lower, sketched.T, lower=True)


def general(field, sketch_one, sketch_two, ranks):
    basis_one = make_basis(field, sketch_one, ranks[0])
    core_one = jnp.einsum("rn,ykn->rky", basis_one, field, precision=HIGHEST)
    regrouped = lax.all_to_all(core_one, "wide", split_axis=0, concat_axis=2, tiled=True)
    basis_two = make_basis(regrouped, sketch_two, ranks[1])
    return jnp.einsum("sn,rkn->rks", basis_two, regrouped, precision=HIGHEST)


def dot(a, b, dims):
    return lax.dot_general(
        a, b, (dims, ((), ())), precision=HIGHEST, preferred_element_type=jnp.float32
    )


NN = ((1,), (0,))
NT = ((1,), (1,))
TN = ((0,), (0,))
BLOCK = 8


def inverse_factor(work, linv):
    size = linv.shape[0]
    tile = (BLOCK, size)
    sub = lax.broadcasted_iota(jnp.int32, tile, 0)

    def body(i, carry):
        r0 = pl.multiple_of(i * BLOCK, BLOCK)
        rows_a = work[pl.ds(r0, BLOCK), :size]
        rows_t = work[pl.ds(r0, BLOCK), size:]
        rolled = pltpu.roll(rows_a, lax.rem(size - r0, size), 1)
        d = {}
        for q in range(BLOCK):
            column = jnp.broadcast_to(rolled[:, q : q + 1], tile)
            for p in range(q, BLOCK):
                d[p, q] = jnp.broadcast_to(column[p : p + 1, :], tile)
        done_a, done_t = [], []
        panel_a = jnp.zeros(tile, jnp.float32)
        panel_t = jnp.zeros(tile, jnp.float32)
        for j in range(BLOCK):
            x = d[j, j]
            y = lax.rsqrt(x)
            y = y * (1.5 - 0.5 * ((x * y) * y))
            for p in range(j + 1, BLOCK):
                d[p, j] = d[p, j] * y
            for q in range(j + 1, BLOCK):
                for p in range(q, BLOCK):
                    d[p, q] = d[p, q] - d[p, j] * d[q, j]
            ra = jnp.broadcast_to(rows_a[j : j + 1, :], tile)
            rt = jnp.broadcast_to(rows_t[j : j + 1, :], tile)
            for k in range(j):
                ra = ra - d[j, k] * done_a[k]
                rt = rt - d[j, k] * done_t[k]
            ra = ra * y
            rt = rt * y
            done_a.append(ra)
            done_t.append(rt)
            panel_a = jnp.where(sub == j, ra, panel_a)
            panel_t = jnp.where(sub == j, rt, panel_t)
        linv[pl.ds(r0, BLOCK), :] = panel_t
        both = jnp.concatenate([panel_a, panel_t], axis=1)
        work[...] = work[...] - dot(panel_a, both, TN)
        return carry

    lax.fori_loop(0, size // BLOCK, body, 0)


def fill_work(work, inner, keep_row, size):
    row = lax.broadcasted_iota(jnp.int32, (size, size), 0)
    col = lax.broadcasted_iota(jnp.int32, (size, size), 1)
    eye = (row == col).astype(jnp.float32)
    work[:, :size] = inner + eye * (1.0 - keep_row)
    work[:, size:] = eye


def kernel(
    n, field, sketch_one, sketch_two, ranks, out,
    flat, part_one, got_one, full_one, work, linv, core, give, have,
    part_two, got_two, full_two, send_sem, recv_sem,
):
    me = lax.axis_index("wide")
    ydev, kdim, n1 = field.shape
    size = sketch_one.shape[1]
    n2 = sketch_two.shape[0]
    stride = flat.shape[0] // ydev
    per = size // n
    c1 = n1 // n
    c2 = n2 // n

    barrier = pltpu.get_barrier_semaphore()

    def greet(i, carry):
        peer = lax.rem(me + 1 + i, n)
        pl.semaphore_signal(barrier, inc=1, device_id={"wide": peer}, device_id_type=MESH)
        return carry

    lax.fori_loop(0, n - 1, greet, 0)

    def exchange(phase, source, target, whole):
        def start(i, carry):
            peer = lax.rem(me + 1 + i, n)
            pltpu.make_async_remote_copy(
                src_ref=source(peer), dst_ref=target(i),
                send_sem=send_sem.at[phase], recv_sem=recv_sem.at[phase],
                device_id={"wide": peer}, device_id_type=MESH,
            ).start()
            return carry

        lax.fori_loop(0, n - 1, start, 0)
        everything = pltpu.make_async_remote_copy(
            src_ref=whole, dst_ref=whole,
            send_sem=send_sem.at[phase], recv_sem=recv_sem.at[phase],
            device_id={"wide": lax.rem(me + 1, n)}, device_id_type=MESH,
        )
        everything.wait_recv()
        everything.wait_send()

    lane = lax.broadcasted_iota(jnp.int32, (1, size), 1)
    keep_one = (lane < ranks[0]).astype(jnp.float32)
    keep_two = (lane < ranks[1]).astype(jnp.float32)

    for y in range(ydev):
        flat[y * stride : y * stride + kdim, :] = field[y]
        flat[y * stride + kdim : (y + 1) * stride, :] = jnp.zeros(
            (stride - kdim, n1), jnp.float32
        )
    projected = dot(flat[...], sketch_one[...] * keep_one, NN)
    part_one[...] = dot(projected, flat[...], TN).T
    masked_two = (sketch_two[...] * keep_two).T

    pl.semaphore_wait(barrier, n - 1)

    exchange(
        0,
        lambda p: part_one.at[pl.ds(pl.multiple_of(p * c1, c1), c1), :],
        lambda i: got_one.at[i],
        got_one,
    )
    mine_one = pl.ds(pl.multiple_of(me * c1, c1), c1)
    full_one[mine_one, :] = jnp.sum(got_one[...], axis=0) + part_one[mine_one, :]
    exchange(
        1,
        lambda p: full_one.at[mine_one, :],
        lambda i: full_one.at[mine_one, :],
        full_one.at[pl.ds(0, n1 - c1), :],
    )
    sk = full_one[...]
    fill_work(work, dot(sk, sk, TN), keep_one, size)
    rotated = dot(flat[...], sk, NN)
    inverse_factor(work, linv)
    mixed = dot(linv[...], rotated, NT)
    for t in range(ydev // 2):
        core[t] = mixed[:, 2 * stride * t : 2 * stride * (t + 1)]

    low = lax.broadcasted_iota(jnp.int32, (n, 2 * stride), 1) < stride
    for half in range(per // 2):
        for t in range(ydev // 2):
            first = core[t, pl.ds(2 * half, n, stride=per), :]
            second = core[t, pl.ds(2 * half + 1, n, stride=per), :]
            even = jnp.where(low, first, pltpu.roll(second, stride, 1))
            odd = jnp.where(low, pltpu.roll(first, stride, 1), second)
            give[half, pl.ds(2 * t, n, stride=ydev), :] = even
            give[half, pl.ds(2 * t + 1, n, stride=ydev), :] = odd
    mine_y = pl.ds(pl.multiple_of(me * ydev, ydev), ydev)
    have[:, mine_y, :] = give[:, mine_y, :]
    exchange(
        2,
        lambda p: give.at[:, pl.ds(pl.multiple_of(p * ydev, ydev), ydev), :],
        lambda i: have.at[:, mine_y, :],
        have.at[:, pl.ds(0, n2 - ydev), :],
    )

    total = jnp.zeros((n2, size), jnp.float32)
    for half in range(per // 2):
        fibers = have[half]
        total = total + dot(fibers, dot(masked_two, fibers, NN), NT)
    part_two[...] = total
    exchange(
        3,
        lambda p: part_two.at[pl.ds(pl.multiple_of(p * c2, c2), c2), :],
        lambda i: got_two.at[i],
        got_two,
    )
    mine_two = pl.ds(pl.multiple_of(me * c2, c2), c2)
    full_two[mine_two, :] = jnp.sum(got_two[...], axis=0) + part_two[mine_two, :]
    exchange(
        4,
        lambda p: full_two.at[mine_two, :],
        lambda i: full_two.at[mine_two, :],
        full_two.at[pl.ds(0, n2 - c2), :],
    )
    sk = full_two[...]
    fill_work(work, dot(sk, sk, TN), keep_two, size)
    spun = [dot(have[half], sk, TN) for half in range(per // 2)]
    inverse_factor(work, linv)
    for half in range(per // 2):
        done = dot(spun[half], linv[...], NT)
        for i in range(2):
            out[2 * half + i] = done[stride * i : stride * i + kdim, :]


def fused(n, field, sketch_one, sketch_two, ranks):
    ydev, kdim, n1 = field.shape
    n2, size = sketch_two.shape
    stride = size // 2
    vmem = pl.BlockSpec(memory_space=pltpu.VMEM)
    f32 = jnp.float32
    return pl.pallas_call(
        functools.partial(kernel, n),
        out_shape=jax.ShapeDtypeStruct((size // n, kdim, size), f32),
        in_specs=[vmem, vmem, vmem, pl.BlockSpec(memory_space=pltpu.SMEM)],
        out_specs=vmem,
        scratch_shapes=[
            pltpu.VMEM((ydev * stride, n1), f32),
            pltpu.VMEM((n1, size), f32),
            pltpu.VMEM((n - 1, n1 // n, size), f32),
            pltpu.VMEM((n1, size), f32),
            pltpu.VMEM((size, 2 * size), f32),
            pltpu.VMEM((size, size), f32),
            pltpu.VMEM((ydev // 2, size, 2 * stride), f32),
            pltpu.VMEM((size // n // 2, n2, size), f32),
            pltpu.VMEM((size // n // 2, n2, size), f32),
            pltpu.VMEM((n2, size), f32),
            pltpu.VMEM((n - 1, n2 // n, size), f32),
            pltpu.VMEM((n2, size), f32),
            pltpu.SemaphoreType.DMA((5,)),
            pltpu.SemaphoreType.DMA((5,)),
        ],
        compiler_params=pltpu.CompilerParams(
            collective_id=0, has_side_effects=True, vmem_limit_bytes=32 * 1024 * 1024
        ),
        cost_estimate=pl.CostEstimate(
            flops=600_000_000, bytes_accessed=2_000_000, transcendentals=256
        ),
    )(field, sketch_one, sketch_two, ranks)


def solution(mesh):
    n = mesh.shape["wide"]

    def per_device(field, sketch_one, sketch_two, ranks):
        ydev, kdim, n1 = field.shape
        n2, size = sketch_two.shape
        fits = (
            mesh.shape["narrow"] == 1
            and size == 128
            and ydev == 8
            and kdim <= size // 2
            and size % (2 * n) == 0
            and n1 % (8 * n) == 0
            and n2 == 8 * n
        )
        if fits:
            return fused(n, field, sketch_one, sketch_two, ranks)
        return general(field, sketch_one, sketch_two, ranks)

    return jax.shard_map(
        per_device,
        mesh=mesh,
        in_specs=(P("wide", "narrow", None), P(), P(), P()),
        out_specs=P("wide", "narrow", None),
        check_vma=False,
    )
```

time: 347 us -> 66.3 us (0.19)
  waiting for transfers between devices: 254 us -> 0 us
  Pallas kernels: 0 us -> 63.9 us
  other arithmetic: 49.5 us -> 0 us
  between operations: 13.6 us -> 0.04 us
  blocking collectives: 12.1 us -> 0 us
  matrix products: 11.5 us -> 0 us
    psum x2 -> x0, waiting for transfers between devices: 254 us -> none  [combine(): return lax.psum(partial_sum, ('wide', 'narrow'))]
    pallas_call x0 -> x1, Pallas kernels: none -> 63.9 us  [fused(): pl.pallas_call(functools.partial(kernel, n), out_shape=jax.ShapeDtypeStru...]
    another operation x10 -> x0, other arithmetic: 45.8 us -> none  [the longest x6 24.9 us: make_basis(): lower = jnp.linalg.cholesky(inner)]
    all_to_all x1 -> x0, blocking collectives: 12.1 us -> none  [per_device(): lax.all_to_all(core_one, 'wide', split_axis=0, concat_axis=2, tiled=True)]
    dot_general x8 -> x0, matrix products: 10.8 us -> none  [the longest x2 4.22 us: make_basis(): partial_gram = jnp.einsum('akn,akm->nm', local, local, precision=highest)]
  transfers between devices with their start and end apart: 2 -> 0, of which waited for: 2 -> 0; matrix products, arithmetic and copies ran while one was open for 1% -> 0% of each run, Pallas kernels for 0% -> 0%
where the time goes in v1:
time: 66.3 us; the launch traced here: 66.2 us
  Pallas kernels  63.9 us (96%)
  local copies, waits for them, and re-layouts  2.27 us (3%)
    pallas_call x1, Pallas kernels, fused(): pl.pallas_call(functools.partial(kernel, n), out_shape=jax.ShapeDtypeStru...  63.9 us
    unnamed x7, local copies, waits for them, and re-layouts  1.59 us

profile of v1, /device:TPU:0, one launch (start us, length us, event | category | flops | bytes accessed | tf_op | source)
XLA Modules:
  0.0 66.2 jit_solution(16897106784780939812)
XLA Ops:
  0.0 0.0 copy-start.2
  0.0 0.0 copy-start.1
  0.0 0.0 copy-start
  0.0 1.6 %copy.5.field = f32[8,44,512]{2,1,0:T(8,128)S(1)} copy(f32[8,44,512]{2,0,1:T(8,128)} %param.4) | data formatting | bytes 1441792 | tf_op args[0]
  1.6 0.0 copy-done.2
  1.6 0.0 copy-done.1
  1.6 0.0 copy-done
  1.6 63.9 %shard_map.46 = f32[4,44,128]{2,1,0:T(8,128)S(1)} custom-call(f32[8,44,512]{2,1,0:T(8,128)S(1)} %copy.5.field, f32[512,128]{1,0:T(8,128)S(1)} %copy-done, f32[256,128]{1,0:T(8,128)S(1)} %copy-done.1, s32[2]{0:T(128)S(1)} %copy-done.2), custom_call_target="tpu_custom_call" | custom-call | flops 600000000 | bytes 2000000 | tf_op jit(solution)/shard_map/pallas_call | solution.py:231
  65.5 0.7 %copy.6 = f32[4,44,128]{2,0,1:T(4,128)} copy(f32[4,44,128]{2,1,0:T(8,128)S(1)} %shard_map.46) | data formatting | bytes 180224 | tf_op jit(solution)/shard_map/pallas_call | solution.py:231
Async XLA Ops:
  0.0 1.6 %copy-start.2 = (s32[2]{0:T(128)S(1)}, s32[2]{0:T(128)}, u32[]{:S(2)}) copy-start(s32[2]{0:T(128)} %ranks.1) | copy-start | bytes 28
  0.0 1.6 %copy-start.1 = (f32[256,128]{1,0:T(8,128)S(1)}, f32[256,128]{1,0:T(8,128)}, u32[]{:S(2)}) copy-start(f32[256,128]{1,0:T(8,128)} %sketch_two.1) | copy-start | bytes 393220
  0.0 1.6 %copy-start = (f32[512,128]{1,0:T(8,128)S(1)}, f32[512,128]{1,0:T(8,128)}, u32[]{:S(2)}) copy-start(f32[512,128]{1,0:T(8,128)} %sketch_one.1) | copy-start | bytes 786436

commit v2 on v1

--- a/solution.py
+++ b/solution.py
@@ -98,8 +98,8 @@
 
 def kernel(
     n, field, sketch_one, sketch_two, ranks, out,
-    flat, part_one, got_one, full_one, work, linv, core, give, have,
-    part_two, got_two, full_two, send_sem, recv_sem,
+    flat, part_one, pair_one, got_one, full_one, work, linv, core, give, have,
+    part_two, pair_two, got_two, full_two, send_sem, recv_sem,
 ):
     me = lax.axis_index("wide")
     ydev, kdim, n1 = field.shape
@@ -107,8 +107,6 @@
     n2 = sketch_two.shape[0]
     stride = flat.shape[0] // ydev
     per = size // n
-    c1 = n1 // n
-    c2 = n2 // n
 
     barrier = pltpu.get_barrier_semaphore()
 
@@ -119,9 +117,22 @@
 
     lax.fori_loop(0, n - 1, greet, 0)
 
-    def exchange(phase, source, target, whole):
+    core_id = lax.rem(me, 2)
+    chip = me // 2
+    chips = n // 2
+
+    def every(i):
+        return lax.rem(me + 1 + i, n)
+
+    def alike(i):
+        return 2 * lax.rem(chip + 1 + i, chips) + core_id
+
+    def twin(i):
+        return chip * 2 + 1 - core_id
+
+    def exchange(phase, count, peer_of, source, target, whole):
         def start(i, carry):
-            peer = lax.rem(me + 1 + i, n)
+            peer = peer_of(i)
             pltpu.make_async_remote_copy(
                 src_ref=source(peer), dst_ref=target(i),
                 send_sem=send_sem.at[phase], recv_sem=recv_sem.at[phase],
@@ -129,14 +140,46 @@
             ).start()
             return carry
 
-        lax.fori_loop(0, n - 1, start, 0)
+        lax.fori_loop(0, count, start, 0)
         everything = pltpu.make_async_remote_copy(
             src_ref=whole, dst_ref=whole,
             send_sem=send_sem.at[phase], recv_sem=recv_sem.at[phase],
-            device_id={"wide": lax.rem(me + 1, n)}, device_id_type=MESH,
+            device_id={"wide": peer_of(0)}, device_id_type=MESH,
         )
         everything.wait_recv()
         everything.wait_send()
+
+    def sum_over_devices(phase, part, pair, got, full):
+        rows = part.shape[0]
+        half = rows // 2
+        chunk = rows // n
+
+        def half_of(device):
+            return pl.ds(pl.multiple_of(lax.rem(device, 2) * half, 8), half)
+
+        def chunk_of(device):
+            start = lax.rem(device, 2) * half + (device // 2) * chunk
+            return pl.ds(pl.multiple_of(start, 8), chunk)
+
+        exchange(phase, 1, twin, lambda p: part.at[half_of(p), :], lambda i: pair, pair)
+        mine = half_of(me)
+        part[mine, :] = part[mine, :] + pair[...]
+        exchange(
+            phase + 1, chips - 1, alike,
+            lambda p: part.at[chunk_of(p), :], lambda i: got.at[i], got,
+        )
+        own = chunk_of(me)
+        full[own, :] = jnp.sum(got[...], axis=0) + part[own, :]
+        exchange(
+            phase + 2, chips - 1, alike,
+            lambda p: full.at[own, :], lambda i: full.at[own, :],
+            full.at[pl.ds(0, half - chunk), :],
+        )
+        exchange(
+            phase + 3, 1, twin,
+            lambda p: full.at[mine, :], lambda i: full.at[mine, :],
+            full.at[pl.ds(0, half), :],
+        )
 
     lane = lax.broadcasted_iota(jnp.int32, (1, size), 1)
     keep_one = (lane < ranks[0]).astype(jnp.float32)
@@ -153,20 +196,7 @@
 
     pl.semaphore_wait(barrier, n - 1)
 
-    exchange(
-        0,
-        lambda p: part_one.at[pl.ds(pl.multiple_of(p * c1, c1), c1), :],
-        lambda i: got_one.at[i],
-        got_one,
-    )
-    mine_one = pl.ds(pl.multiple_of(me * c1, c1), c1)
-    full_one[mine_one, :] = jnp.sum(got_one[...], axis=0) + part_one[mine_one, :]
-    exchange(
-        1,
-        lambda p: full_one.at[mine_one, :],
-        lambda i: full_one.at[mine_one, :],
-        full_one.at[pl.ds(0, n1 - c1), :],
-    )
+    sum_over_devices(0, part_one, pair_one, got_one, full_one)
     sk = full_one[...]
     fill_work(work, dot(sk, sk, TN), keep_one, size)
     rotated = dot(flat[...], sk, NN)
@@ -187,7 +217,7 @@
     mine_y = pl.ds(pl.multiple_of(me * ydev, ydev), ydev)
     have[:, mine_y, :] = give[:, mine_y, :]
     exchange(
-        2,
+        8, n - 1, every,
         lambda p: give.at[:, pl.ds(pl.multiple_of(p * ydev, ydev), ydev), :],
         lambda i: have.at[:, mine_y, :],
         have.at[:, pl.ds(0, n2 - ydev), :],
@@ -198,20 +228,7 @@
         fibers = have[half]
         total = total + dot(fibers, dot(masked_two, fibers, NN), NT)
     part_two[...] = total
-    exchange(
-        3,
-        lambda p: part_two.at[pl.ds(pl.multiple_of(p * c2, c2), c2), :],
-        lambda i: got_two.at[i],
-        got_two,
-    )
-    mine_two = pl.ds(pl.multiple_of(me * c2, c2), c2)
-    full_two[mine_two, :] = jnp.sum(got_two[...], axis=0) + part_two[mine_two, :]
-    exchange(
-        4,
-        lambda p: full_two.at[mine_two, :],
-        lambda i: full_two.at[mine_two, :],
-        full_two.at[pl.ds(0, n2 - c2), :],
-    )
+    sum_over_devices(4, part_two, pair_two, got_two, full_two)
     sk = full_two[...]
     fill_work(work, dot(sk, sk, TN), keep_two, size)
     spun = [dot(have[half], sk, TN) for half in range(per // 2)]
@@ -236,7 +253,8 @@
         scratch_shapes=[
             pltpu.VMEM((ydev * stride, n1), f32),
             pltpu.VMEM((n1, size), f32),
-            pltpu.VMEM((n - 1, n1 // n, size), f32),
+            pltpu.VMEM((n1 // 2, size), f32),
+            pltpu.VMEM((n // 2 - 1, n1 // n, size), f32),
             pltpu.VMEM((n1, size), f32),
             pltpu.VMEM((size, 2 * size), f32),
             pltpu.VMEM((size, size), f32),
@@ -244,10 +262,11 @@
             pltpu.VMEM((size // n // 2, n2, size), f32),
             pltpu.VMEM((size // n // 2, n2, size), f32),
             pltpu.VMEM((n2, size), f32),
-            pltpu.VMEM((n - 1, n2 // n, size), f32),
+            pltpu.VMEM((n2 // 2, size), f32),
+            pltpu.VMEM((n // 2 - 1, n2 // n, size), f32),
             pltpu.VMEM((n2, size), f32),
-            pltpu.SemaphoreType.DMA((5,)),
-            pltpu.SemaphoreType.DMA((5,)),
+            pltpu.SemaphoreType.DMA((9,)),
+            pltpu.SemaphoreType.DMA((9,)),
         ],
         compiler_params=pltpu.CompilerParams(
             collective_id=0, has_side_effects=True, vmem_limit_bytes=32 * 1024 * 1024
@@ -267,6 +286,8 @@
         fits = (
             mesh.shape["narrow"] == 1
             and size == 128
+            and n % 2 == 0
+            and n >= 4
             and ydev == 8
             and kdim <= size // 2
             and size % (2 * n) == 0

time: 66.3 us -> 64.6 us (0.974)
  Pallas kernels: 63.9 us -> 62.1 us
    pallas_call x1, Pallas kernels: 63.9 us -> 62.1 us  [fused(): pl.pallas_call(functools.partial(kernel, n), out_shape=jax.ShapeDtypeStru...]
where the time goes in v2:
time: 64.6 us; the launch traced here: 64.4 us
  Pallas kernels  62.1 us (96%)
  local copies, waits for them, and re-layouts  2.27 us (4%)
    pallas_call x1, Pallas kernels, fused(): pl.pallas_call(functools.partial(kernel, n), out_shape=jax.ShapeDtypeStru...  62.1 us
    unnamed x7, local copies, waits for them, and re-layouts  1.59 us

profile of v2, /device:TPU:0, one launch (start us, length us, event | category | flops | bytes accessed | tf_op | source)
XLA Modules:
  0.0 64.4 jit_solution(10813935901595404335)
XLA Ops:
  0.0 0.0 copy-start.2
  0.0 0.0 copy-start.1
  0.0 0.0 copy-start
  0.0 1.6 %copy.5.field = f32[8,44,512]{2,1,0:T(8,128)S(1)} copy(f32[8,44,512]{2,0,1:T(8,128)} %param.4) | data formatting | bytes 1441792 | tf_op args[0]
  1.6 0.0 copy-done.2
  1.6 0.0 copy-done.1
  1.6 0.0 copy-done
  1.6 62.1 %shard_map.46 = f32[4,44,128]{2,1,0:T(8,128)S(1)} custom-call(f32[8,44,512]{2,1,0:T(8,128)S(1)} %copy.5.field, f32[512,128]{1,0:T(8,128)S(1)} %copy-done, f32[256,128]{1,0:T(8,128)S(1)} %copy-done.1, s32[2]{0:T(128)S(1)} %copy-done.2), custom_call_target="tpu_custom_call" | custom-call | flops 600000000 | bytes 2000000 | tf_op jit(solution)/shard_map/pallas_call | solution.py:248
  63.7 0.7 %copy.6 = f32[4,44,128]{2,0,1:T(4,128)} copy(f32[4,44,128]{2,1,0:T(8,128)S(1)} %shard_map.46) | data formatting | bytes 180224 | tf_op jit(solution)/shard_map/pallas_call | solution.py:248
Async XLA Ops:
  0.0 1.6 %copy-start.2 = (s32[2]{0:T(128)S(1)}, s32[2]{0:T(128)}, u32[]{:S(2)}) copy-start(s32[2]{0:T(128)} %ranks.1) | copy-start | bytes 28
  0.0 1.6 %copy-start.1 = (f32[256,128]{1,0:T(8,128)S(1)}, f32[256,128]{1,0:T(8,128)}, u32[]{:S(2)}) copy-start(f32[256,128]{1,0:T(8,128)} %sketch_two.1) | copy-start | bytes 393220
  0.0 1.6 %copy-start = (f32[512,128]{1,0:T(8,128)S(1)}, f32[512,128]{1,0:T(8,128)}, u32[]{:S(2)}) copy-start(f32[512,128]{1,0:T(8,128)} %sketch_one.1) | copy-start | bytes 786436

commit v3 on v2

--- a/solution.py
+++ b/solution.py
@@ -40,52 +40,73 @@
 NT = ((1,), (1,))
 TN = ((0,), (0,))
 BLOCK = 8
+TILES = 4
 
 
 def inverse_factor(work, linv):
     size = linv.shape[0]
     tile = (BLOCK, size)
+    group = TILES * BLOCK
     sub = lax.broadcasted_iota(jnp.int32, tile, 0)
 
     def body(i, carry):
-        r0 = pl.multiple_of(i * BLOCK, BLOCK)
-        rows_a = work[pl.ds(r0, BLOCK), :size]
-        rows_t = work[pl.ds(r0, BLOCK), size:]
-        rolled = pltpu.roll(rows_a, lax.rem(size - r0, size), 1)
-        d = {}
-        for q in range(BLOCK):
-            column = jnp.broadcast_to(rolled[:, q : q + 1], tile)
-            for p in range(q, BLOCK):
-                d[p, q] = jnp.broadcast_to(column[p : p + 1, :], tile)
-        done_a, done_t = [], []
-        panel_a = jnp.zeros(tile, jnp.float32)
-        panel_t = jnp.zeros(tile, jnp.float32)
-        for j in range(BLOCK):
-            x = d[j, j]
-            y = lax.rsqrt(x)
-            y = y * (1.5 - 0.5 * ((x * y) * y))
-            for p in range(j + 1, BLOCK):
-                d[p, j] = d[p, j] * y
-            for q in range(j + 1, BLOCK):
+        r0 = pl.multiple_of(i * group, group)
+        rolled = pltpu.roll(
+            work[pl.ds(r0, group), :size], lax.rem(size - r0, size), 1
+        )
+        rest = work[pl.ds(r0, group), size:]
+        rows_a = [rolled[u * BLOCK : (u + 1) * BLOCK, :] for u in range(TILES)]
+        rows_t = [rest[u * BLOCK : (u + 1) * BLOCK, :] for u in range(TILES)]
+        panels_a, panels_t = [], []
+        for u in range(TILES):
+            d, below = {}, {}
+            for q in range(BLOCK):
+                lane = u * BLOCK + q
+                column = jnp.broadcast_to(rows_a[u][:, lane : lane + 1], tile)
                 for p in range(q, BLOCK):
-                    d[p, q] = d[p, q] - d[p, j] * d[q, j]
-            ra = jnp.broadcast_to(rows_a[j : j + 1, :], tile)
-            rt = jnp.broadcast_to(rows_t[j : j + 1, :], tile)
-            for k in range(j):
-                ra = ra - d[j, k] * done_a[k]
-                rt = rt - d[j, k] * done_t[k]
-            ra = ra * y
-            rt = rt * y
-            done_a.append(ra)
-            done_t.append(rt)
-            panel_a = jnp.where(sub == j, ra, panel_a)
-            panel_t = jnp.where(sub == j, rt, panel_t)
-        linv[pl.ds(r0, BLOCK), :] = panel_t
+                    d[p, q] = jnp.broadcast_to(column[p : p + 1, :], tile)
+                for v in range(u + 1, TILES):
+                    below[v, q] = jnp.broadcast_to(rows_a[v][:, lane : lane + 1], tile)
+            done_a, done_t = [], []
+            panel_a = jnp.zeros(tile, jnp.float32)
+            panel_t = jnp.zeros(tile, jnp.float32)
+            for j in range(BLOCK):
+                x = d[j, j]
+                y = lax.rsqrt(x)
+                y = y * (1.5 - 0.5 * ((x * y) * y))
+                for p in range(j + 1, BLOCK):
+                    d[p, j] = d[p, j] * y
+                for v in range(u + 1, TILES):
+                    below[v, j] = below[v, j] * y
+                for q in range(j + 1, BLOCK):
+                    for p in range(q, BLOCK):
+                        d[p, q] = d[p, q] - d[p, j] * d[q, j]
+                    for v in range(u + 1, TILES):
+                        below[v, q] = below[v, q] - below[v, j] * d[q, j]
+                ra = jnp.broadcast_to(rows_a[u][j : j + 1, :], tile)
+                rt = jnp.broadcast_to(rows_t[u][j : j + 1, :], tile)
+                for k in range(j):
+                    ra = ra - d[j, k] * done_a[k]
+                    rt = rt - d[j, k] * done_t[k]
+                ra = ra * y
+                rt = rt * y
+                done_a.append(ra)
+                done_t.append(rt)
+                panel_a = jnp.where(sub == j, ra, panel_a)
+                panel_t = jnp.where(sub == j, rt, panel_t)
+                for v in range(u + 1, TILES):
+                    rows_a[v] = rows_a[v] - below[v, j] * ra
+                    rows_t[v] = rows_t[v] - below[v, j] * rt
+            panels_a.append(panel_a)
+            panels_t.append(panel_t)
+        panel_t = jnp.concatenate(panels_t, axis=0)
+        panel_a = pltpu.roll(jnp.concatenate(panels_a, axis=0), r0, 1)
+        linv[pl.ds(r0, group), :] = panel_t
         both = jnp.concatenate([panel_a, panel_t], axis=1)
         work[...] = work[...] - dot(panel_a, both, TN)
         return carry
 
-    lax.fori_loop(0, size // BLOCK, body, 0)
+    lax.fori_loop(0, size // group, body, 0)
 
 
 def fill_work(work, inner, keep_row, size):

time: 64.6 us -> 57.2 us (0.89)
  Pallas kernels: 62.1 us -> 54.7 us
    pallas_call x1, Pallas kernels: 62.1 us -> 54.7 us  [fused(): pl.pallas_call(functools.partial(kernel, n), out_shape=jax.ShapeDtypeStru...]
where the time goes in v3:
time: 57.2 us; the launch traced here: 57 us
  Pallas kernels  54.7 us (96%)
  local copies, waits for them, and re-layouts  2.27 us (4%)
    pallas_call x1, Pallas kernels, fused(): pl.pallas_call(functools.partial(kernel, n), out_shape=jax.ShapeDtypeStru...  54.7 us
    unnamed x7, local copies, waits for them, and re-layouts  1.59 us

profile of v3, /device:TPU:0, one launch (start us, length us, event | category | flops | bytes accessed | tf_op | source)
XLA Modules:
  0.0 57.0 jit_solution(8485162435928251844)
XLA Ops:
  0.0 0.0 copy-start.2
  0.0 0.0 copy-start.1
  0.0 0.0 copy-start
  0.0 1.6 %copy.5.field = f32[8,44,512]{2,1,0:T(8,128)S(1)} copy(f32[8,44,512]{2,0,1:T(8,128)} %param.4) | data formatting | bytes 1441792 | tf_op args[0]
  1.6 0.0 copy-done.2
  1.6 0.0 copy-done.1
  1.6 0.0 copy-done
  1.6 54.7 %shard_map.46 = f32[4,44,128]{2,1,0:T(8,128)S(1)} custom-call(f32[8,44,512]{2,1,0:T(8,128)S(1)} %copy.5.field, f32[512,128]{1,0:T(8,128)S(1)} %copy-done, f32[256,128]{1,0:T(8,128)S(1)} %copy-done.1, s32[2]{0:T(128)S(1)} %copy-done.2), custom_call_target="tpu_custom_call" | custom-call | flops 600000000 | bytes 2000000 | tf_op jit(solution)/shard_map/pallas_call | solution.py:269
  56.3 0.7 %copy.6 = f32[4,44,128]{2,0,1:T(4,128)} copy(f32[4,44,128]{2,1,0:T(8,128)S(1)} %shard_map.46) | data formatting | bytes 180224 | tf_op jit(solution)/shard_map/pallas_call | solution.py:269
Async XLA Ops:
  0.0 1.6 %copy-start.2 = (s32[2]{0:T(128)S(1)}, s32[2]{0:T(128)}, u32[]{:S(2)}) copy-start(s32[2]{0:T(128)} %ranks.1) | copy-start | bytes 28
  0.0 1.6 %copy-start.1 = (f32[256,128]{1,0:T(8,128)S(1)}, f32[256,128]{1,0:T(8,128)}, u32[]{:S(2)}) copy-start(f32[256,128]{1,0:T(8,128)} %sketch_two.1) | copy-start | bytes 393220
  0.0 1.6 %copy-start = (f32[512,128]{1,0:T(8,128)S(1)}, f32[512,128]{1,0:T(8,128)}, u32[]{:S(2)}) copy-start(f32[512,128]{1,0:T(8,128)} %sketch_one.1) | copy-start | bytes 786436

commit v4 on v3

--- a/solution.py
+++ b/solution.py
@@ -49,19 +49,16 @@
     group = TILES * BLOCK
     sub = lax.broadcasted_iota(jnp.int32, tile, 0)
 
-    def body(i, carry):
-        r0 = pl.multiple_of(i * group, group)
-        rolled = pltpu.roll(
-            work[pl.ds(r0, group), :size], lax.rem(size - r0, size), 1
-        )
-        rest = work[pl.ds(r0, group), size:]
-        rows_a = [rolled[u * BLOCK : (u + 1) * BLOCK, :] for u in range(TILES)]
+    for r0 in range(0, size, group):
+        own = work[r0 : r0 + group, :size]
+        rest = work[r0 : r0 + group, size:]
+        rows_a = [own[u * BLOCK : (u + 1) * BLOCK, :] for u in range(TILES)]
         rows_t = [rest[u * BLOCK : (u + 1) * BLOCK, :] for u in range(TILES)]
         panels_a, panels_t = [], []
         for u in range(TILES):
             d, below = {}, {}
             for q in range(BLOCK):
-                lane = u * BLOCK + q
+                lane = r0 + u * BLOCK + q
                 column = jnp.broadcast_to(rows_a[u][:, lane : lane + 1], tile)
                 for p in range(q, BLOCK):
                     d[p, q] = jnp.broadcast_to(column[p : p + 1, :], tile)
@@ -100,13 +97,12 @@
             panels_a.append(panel_a)
             panels_t.append(panel_t)
         panel_t = jnp.concatenate(panels_t, axis=0)
-        panel_a = pltpu.roll(jnp.concatenate(panels_a, axis=0), r0, 1)
-        linv[pl.ds(r0, group), :] = panel_t
-        both = jnp.concatenate([panel_a, panel_t], axis=1)
-        work[...] = work[...] - dot(panel_a, both, TN)
-        return carry
-
-    lax.fori_loop(0, size // group, body, 0)
+        panel_a = jnp.concatenate(panels_a, axis=0)
+        linv[r0 : r0 + group, :] = panel_t
+        end = r0 + group
+        if end < size:
+            both = jnp.concatenate([panel_a, panel_t], axis=1)
+            work[end:, :] = work[end:, :] - dot(panel_a.T[end:, :], both, NN)
 
 
 def fill_work(work, inner, keep_row, size):
@@ -170,7 +166,7 @@
         everything.wait_recv()
         everything.wait_send()
 
-    def sum_over_devices(phase, part, pair, got, full):
+    def sum_over_devices(phase, part, pair, got, full, direct):
         rows = part.shape[0]
         half = rows // 2
         chunk = rows // n
@@ -191,6 +187,13 @@
         )
         own = chunk_of(me)
         full[own, :] = jnp.sum(got[...], axis=0) + part[own, :]
+        if direct:
+            exchange(
+                phase + 2, n - 1, every,
+                lambda p: full.at[own, :], lambda i: full.at[own, :],
+                full.at[pl.ds(0, rows - chunk), :],
+            )
+            return
         exchange(
             phase + 2, chips - 1, alike,
             lambda p: full.at[own, :], lambda i: full.at[own, :],
@@ -217,7 +220,7 @@
 
     pl.semaphore_wait(barrier, n - 1)
 
-    sum_over_devices(0, part_one, pair_one, got_one, full_one)
+    sum_over_devices(0, part_one, pair_one, got_one, full_one, False)
     sk = full_one[...]
     fill_work(work, dot(sk, sk, TN), keep_one, size)
     rotated = dot(flat[...], sk, NN)
@@ -249,7 +252,7 @@
         fibers = have[half]
         total = total + dot(fibers, dot(masked_two, fibers, NN), NT)
     part_two[...] = total
-    sum_over_devices(4, part_two, pair_two, got_two, full_two)
+    sum_over_devices(4, part_two, pair_two, got_two, full_two, True)
     sk = full_two[...]
     fill_work(work, dot(sk, sk, TN), keep_two, size)
     spun = [dot(have[half], sk, TN) for half in range(per // 2)]

time: 57.2 us -> 53.4 us (0.934)
  Pallas kernels: 54.7 us -> 50.9 us
    pallas_call x1, Pallas kernels: 54.7 us -> 50.9 us  [fused(): pl.pallas_call(functools.partial(kernel, n), out_shape=jax.ShapeDtypeStru...]
where the time goes in v4:
time: 53.4 us; the launch traced here: 53.2 us
  Pallas kernels  50.9 us (95%)
  local copies, waits for them, and re-layouts  2.27 us (4%)
    pallas_call x1, Pallas kernels, fused(): pl.pallas_call(functools.partial(kernel, n), out_shape=jax.ShapeDtypeStru...  50.9 us
    unnamed x7, local copies, waits for them, and re-layouts  1.59 us

profile of v4, /device:TPU:0, one launch (start us, length us, event | category | flops | bytes accessed | tf_op | source)
XLA Modules:
  0.0 53.2 jit_solution(11028414127946319123)
XLA Ops:
  0.0 0.0 copy-start.2
  0.0 0.0 copy-start.1
  0.0 0.0 copy-start
  0.0 1.6 %copy.5.field = f32[8,44,512]{2,1,0:T(8,128)S(1)} copy(f32[8,44,512]{2,0,1:T(8,128)} %param.4) | data formatting | bytes 1441792 | tf_op args[0]
  1.6 0.0 copy-done.2
  1.6 0.0 copy-done.1
  1.6 0.0 copy-done
  1.6 50.9 %shard_map.46 = f32[4,44,128]{2,1,0:T(8,128)S(1)} custom-call(f32[8,44,512]{2,1,0:T(8,128)S(1)} %copy.5.field, f32[512,128]{1,0:T(8,128)S(1)} %copy-done, f32[256,128]{1,0:T(8,128)S(1)} %copy-done.1, s32[2]{0:T(128)S(1)} %copy-done.2), custom_call_target="tpu_custom_call" | custom-call | flops 600000000 | bytes 2000000 | tf_op jit(solution)/shard_map/pallas_call | solution.py:272
  52.6 0.7 %copy.6 = f32[4,44,128]{2,0,1:T(4,128)} copy(f32[4,44,128]{2,1,0:T(8,128)S(1)} %shard_map.46) | data formatting | bytes 180224 | tf_op jit(solution)/shard_map/pallas_call | solution.py:272
Async XLA Ops:
  0.0 1.6 %copy-start.2 = (s32[2]{0:T(128)S(1)}, s32[2]{0:T(128)}, u32[]{:S(2)}) copy-start(s32[2]{0:T(128)} %ranks.1) | copy-start | bytes 28
  0.0 1.6 %copy-start.1 = (f32[256,128]{1,0:T(8,128)S(1)}, f32[256,128]{1,0:T(8,128)}, u32[]{:S(2)}) copy-start(f32[256,128]{1,0:T(8,128)} %sketch_two.1) | copy-start | bytes 393220
  0.0 1.6 %copy-start = (f32[512,128]{1,0:T(8,128)S(1)}, f32[512,128]{1,0:T(8,128)}, u32[]{:S(2)}) copy-start(f32[512,128]{1,0:T(8,128)} %sketch_one.1) | copy-start | bytes 786436

commit v5 on v4

--- a/solution.py
+++ b/solution.py
@@ -40,7 +40,7 @@
 NT = ((1,), (1,))
 TN = ((0,), (0,))
 BLOCK = 8
-TILES = 4
+TILES = 8
 
 
 def inverse_factor(work, linv):

time: 53.4 us -> 53.5 us (level)
  no operation moved by 1% of the time
where the time goes in v5:
time: 53.5 us; the launch traced here: 53.4 us
  Pallas kernels  51.1 us (96%)
  local copies, waits for them, and re-layouts  2.27 us (4%)
    pallas_call x1, Pallas kernels, fused(): pl.pallas_call(functools.partial(kernel, n), out_shape=jax.ShapeDtypeStru...  51.1 us
    unnamed x7, local copies, waits for them, and re-layouts  1.59 us

profile of v5, /device:TPU:0, one launch (start us, length us, event | category | flops | bytes accessed | tf_op | source)
XLA Modules:
  0.0 53.4 jit_solution(8031729291091440629)
XLA Ops:
  0.0 0.0 copy-start.2
  0.0 0.0 copy-start.1
  0.0 0.0 copy-start
  0.0 1.6 %copy.5.field = f32[8,44,512]{2,1,0:T(8,128)S(1)} copy(f32[8,44,512]{2,0,1:T(8,128)} %param.4) | data formatting | bytes 1441792 | tf_op args[0]
  1.6 0.0 copy-done.2
  1.6 0.0 copy-done.1
  1.6 0.0 copy-done
  1.6 51.1 %shard_map.46 = f32[4,44,128]{2,1,0:T(8,128)S(1)} custom-call(f32[8,44,512]{2,1,0:T(8,128)S(1)} %copy.5.field, f32[512,128]{1,0:T(8,128)S(1)} %copy-done, f32[256,128]{1,0:T(8,128)S(1)} %copy-done.1, s32[2]{0:T(128)S(1)} %copy-done.2), custom_call_target="tpu_custom_call" | custom-call | flops 600000000 | bytes 2000000 | tf_op jit(solution)/shard_map/pallas_call | solution.py:272
  52.7 0.7 %copy.6 = f32[4,44,128]{2,0,1:T(4,128)} copy(f32[4,44,128]{2,1,0:T(8,128)S(1)} %shard_map.46) | data formatting | bytes 180224 | tf_op jit(solution)/shard_map/pallas_call | solution.py:272
Async XLA Ops:
  0.0 1.6 %copy-start.2 = (s32[2]{0:T(128)S(1)}, s32[2]{0:T(128)}, u32[]{:S(2)}) copy-start(s32[2]{0:T(128)} %ranks.1) | copy-start | bytes 28
  0.0 1.6 %copy-start.1 = (f32[256,128]{1,0:T(8,128)S(1)}, f32[256,128]{1,0:T(8,128)}, u32[]{:S(2)}) copy-start(f32[256,128]{1,0:T(8,128)} %sketch_two.1) | copy-start | bytes 393220
  0.0 1.6 %copy-start = (f32[512,128]{1,0:T(8,128)S(1)}, f32[512,128]{1,0:T(8,128)}, u32[]{:S(2)}) copy-start(f32[512,128]{1,0:T(8,128)} %sketch_one.1) | copy-start | bytes 786436

commit v6 on v4

--- a/solution.py
+++ b/solution.py
@@ -116,7 +116,7 @@
 def kernel(
     n, field, sketch_one, sketch_two, ranks, out,
     flat, part_one, pair_one, got_one, full_one, work, linv, core, give, have,
-    part_two, pair_two, got_two, full_two, send_sem, recv_sem,
+    part_two, got_two, full_two, send_sem, recv_sem,
 ):
     me = lax.axis_index("wide")
     ydev, kdim, n1 = field.shape
@@ -178,13 +178,19 @@
             start = lax.rem(device, 2) * half + (device // 2) * chunk
             return pl.ds(pl.multiple_of(start, 8), chunk)
 
-        exchange(phase, 1, twin, lambda p: part.at[half_of(p), :], lambda i: pair, pair)
         mine = half_of(me)
-        part[mine, :] = part[mine, :] + pair[...]
-        exchange(
-            phase + 1, chips - 1, alike,
-            lambda p: part.at[chunk_of(p), :], lambda i: got.at[i], got,
-        )
+        if direct:
+            exchange(
+                phase, n - 1, every,
+                lambda p: part.at[chunk_of(p), :], lambda i: got.at[i], got,
+            )
+        else:
+            exchange(phase, 1, twin, lambda p: part.at[half_of(p), :], lambda i: pair, pair)
+            part[mine, :] = part[mine, :] + pair[...]
+            exchange(
+                phase + 1, chips - 1, alike,
+                lambda p: part.at[chunk_of(p), :], lambda i: got.at[i], got,
+            )
         own = chunk_of(me)
         full[own, :] = jnp.sum(got[...], axis=0) + part[own, :]
         if direct:
@@ -252,7 +258,7 @@
         fibers = have[half]
         total = total + dot(fibers, dot(masked_two, fibers, NN), NT)
     part_two[...] = total
-    sum_over_devices(4, part_two, pair_two, got_two, full_two, True)
+    sum_over_devices(4, part_two, None, got_two, full_two, True)
     sk = full_two[...]
     fill_work(work, dot(sk, sk, TN), keep_two, size)
     spun = [dot(have[half], sk, TN) for half in range(per // 2)]
@@ -286,8 +292,7 @@
             pltpu.VMEM((size // n // 2, n2, size), f32),
             pltpu.VMEM((size // n // 2, n2, size), f32),
             pltpu.VMEM((n2, size), f32),
-            pltpu.VMEM((n2 // 2, size), f32),
-            pltpu.VMEM((n // 2 - 1, n2 // n, size), f32),
+            pltpu.VMEM((n - 1, n2 // n, size), f32),
             pltpu.VMEM((n2, size), f32),
             pltpu.SemaphoreType.DMA((9,)),
             pltpu.SemaphoreType.DMA((9,)),

time: 53.4 us -> 53.7 us (level)
  no operation moved by 1% of the time
where the time goes in v6:
time: 53.7 us; the launch traced here: 53.6 us
  Pallas kernels  51.3 us (96%)
  local copies, waits for them, and re-layouts  2.27 us (4%)
    pallas_call x1, Pallas kernels, fused(): pl.pallas_call(functools.partial(kernel, n), out_shape=jax.ShapeDtypeStru...  51.3 us
    unnamed x7, local copies, waits for them, and re-layouts  1.59 us

profile of v6, /device:TPU:0, one launch (start us, length us, event | category | flops | bytes accessed | tf_op | source)
XLA Modules:
  0.0 53.6 jit_solution(14898952817905210323)
XLA Ops:
  0.0 0.0 copy-start.2
  0.0 0.0 copy-start.1
  0.0 0.0 copy-start
  0.0 1.6 %copy.5.field = f32[8,44,512]{2,1,0:T(8,128)S(1)} copy(f32[8,44,512]{2,0,1:T(8,128)} %param.4) | data formatting | bytes 1441792 | tf_op args[0]
  1.6 0.0 copy-done.2
  1.6 0.0 copy-done.1
  1.6 0.0 copy-done
  1.6 51.3 %shard_map.46 = f32[4,44,128]{2,1,0:T(8,128)S(1)} custom-call(f32[8,44,512]{2,1,0:T(8,128)S(1)} %copy.5.field, f32[512,128]{1,0:T(8,128)S(1)} %copy-done, f32[256,128]{1,0:T(8,128)S(1)} %copy-done.1, s32[2]{0:T(128)S(1)} %copy-done.2), custom_call_target="tpu_custom_call" | custom-call | flops 600000000 | bytes 2000000 | tf_op jit(solution)/shard_map/pallas_call | solution.py:278
  52.9 0.7 %copy.6 = f32[4,44,128]{2,0,1:T(4,128)} copy(f32[4,44,128]{2,1,0:T(8,128)S(1)} %shard_map.46) | data formatting | bytes 180224 | tf_op jit(solution)/shard_map/pallas_call | solution.py:278
Async XLA Ops:
  0.0 1.6 %copy-start.2 = (s32[2]{0:T(128)S(1)}, s32[2]{0:T(128)}, u32[]{:S(2)}) copy-start(s32[2]{0:T(128)} %ranks.1) | copy-start | bytes 28
  0.0 1.6 %copy-start.1 = (f32[256,128]{1,0:T(8,128)S(1)}, f32[256,128]{1,0:T(8,128)}, u32[]{:S(2)}) copy-start(f32[256,128]{1,0:T(8,128)} %sketch_two.1) | copy-start | bytes 393220
  0.0 1.6 %copy-start = (f32[512,128]{1,0:T(8,128)S(1)}, f32[512,128]{1,0:T(8,128)}, u32[]{:S(2)}) copy-start(f32[512,128]{1,0:T(8,128)} %sketch_one.1) | copy-start | bytes 786436
